TPU v7x, 512 devices: a whole 4x8x8 slice. The times are simulated.
512 devices in a mesh: occ: 64 (over z_lo, y, core), aux: 8 (over z_hi, x).
Axes of the slice: x: 4, y: 8, z: 8 (z_hi: 2, z_lo: 4; z = z_hi * 4 + z_lo), core: 2. Of those that a mesh axis runs over, the one named last changes fastest.
Arguments:
- ints_b: bfloat16 [64, 1024, 5120], P('occ', None, 'aux'), may hold values from -0.69921875 to 0.69921875
- occ_energy: float32 [64], P('occ'), may hold values from -2 to -0.4
- virt_energy: float32 [1024], replicated, may hold values from 0.2 to 3
Outputs:
- gamma_grad: float32 [64, 1024, 5120], P('occ', None, 'aux')
All inputs are finite; a program needn't handle non-finite values.
Results may differ from a plain program's by a relative error of at most 0.015.
Values may be sent and summed in bfloat16 or wider, within the bound.
A program may use at most 64 MiB of HBM per device.

v0:
```python
import jax
import jax.numpy as jnp
from jax import lax
from jax.sharding import PartitionSpec as P


def from_behind(shard, axis, by):
    count = lax.axis_size(axis)
    return lax.ppermute(shard, axis, [(i, (i + by) % count) for i in range(count)])


def denominator(emine, eother, row_energy, col_energy):
    return (
        emine[:, None, None, None]
        + eother[None, :, None, None]
        - row_energy[None, None, :, None]
        - col_energy[None, None, None, :]
    )


def pair_amplitude(ints_b, occ_energy, virt_energy, other, eother):
    partial_value = jnp.einsum("iap,jbp->ijab", ints_b, other, preferred_element_type=jnp.float32)
    coulomb = lax.psum(partial_value.astype(jnp.bfloat16), "aux").astype(jnp.float32)
    amplitude = (coulomb / denominator(occ_energy, eother, virt_energy, virt_energy)).astype(
        jnp.bfloat16
    )
    return amplitude


def gradient_term(amplitude, other):
    return jnp.einsum("ijab,jbp->iap", amplitude, other, preferred_element_type=jnp.float32)


def per_device(ints_b, occ_energy, virt_energy):
    upper = (
        from_behind(ints_b, "occ", -1),
        from_behind(occ_energy.astype(jnp.bfloat16), "occ", -1).astype(occ_energy.dtype),
    )
    lower = (
        from_behind(ints_b, "occ", 1),
        from_behind(occ_energy.astype(jnp.bfloat16), "occ", 1).astype(occ_energy.dtype),
    )
    total = jnp.zeros(ints_b.shape, jnp.float32)
    for neighbour in (upper, lower):
        amplitude = pair_amplitude(ints_b, occ_energy, virt_energy, neighbour[0], neighbour[1])
        total = total + gradient_term(amplitude, neighbour[0])
    return total


def solution(mesh):
    placed = (P("occ", None, "aux"), P("occ"), P())
    return jax.shard_map(
        per_device, mesh=mesh, in_specs=placed, out_specs=P("occ", None, "aux"), check_vma=False
    )
```

profile of v0, /device:TPU:1, one launch (start us, length us, event | category | flops | bytes accessed | tf_op | source)
XLA Modules:
  0.0 260.0 jit_solution(5303478578535004122)
XLA Ops:
  6.5 0.0 copy-start.2
  6.5 0.0 all-reduce.3.cloned.1.call-start
  6.5 4.7 %collective-permute-start.2 = (bf16[1,1024,640]{2,1,0:T(8,128)(2,1)}, bf16[1,1024,640]{2,1,0:T(8,128)(2,1)S(1)}, u32[]{:S(2)}, u32[]{:S(2)}) collective-permute-start(bf16[1,1024,640]{2,1,0:T(8,128)(2,1)} %param.3), channel_id=1, source_target_pairs={{0,8},{8,16},{16,24},{24,32},{32,40},{40,48},{48,56},{56,64},{64,7... | collective-permute-start | bytes 3932168 | tf_op jit(solution)/shard_map/ppermute | solution.py:9
  11.3 6.1 %collective-permute-start = (bf16[1,1024,640]{2,1,0:T(8,128)(2,1)}, bf16[1,1024,640]{2,1,0:T(8,128)(2,1)S(1)}, u32[]{:S(2)}, u32[]{:S(2)}) collective-permute-start(bf16[1,1024,640]{2,1,0:T(8,128)(2,1)} %param.3), channel_id=1, source_target_pairs={{0,504},{8,0},{16,8},{24,16},{32,24},{40,32},{48,40},{56,48},{64,5... | collective-permute-start | bytes 3932168 | tf_op jit(solution)/shard_map/ppermute | solution.py:9
  17.4 8.7 %collective-permute-done.2 = bf16[1,1024,640]{2,1,0:T(8,128)(2,1)S(1)} collective-permute-done((bf16[1,1024,640]{2,1,0:T(8,128)(2,1)}, bf16[1,1024,640]{2,1,0:T(8,128)(2,1)S(1)}, u32[]{:S(2)}, u32[]{:S(2)}) %collective-permute-start.2) | collective-permute-done | bytes 1310752 | tf_op jit(solution)/shard_map/ppermute | solution.py:9
  26.1 0.0 copy-start.3
  26.1 4.9 %convert_bitcast_fusion = bf16[1,1,1024,1024]{2,3,0,1:T(8,128)(2,1)} fusion(bf16[1,1024,640]{2,1,0:T(8,128)(2,1)S(1)} %collective-permute-done.2, bf16[1,1024,640]{2,1,0:T(8,128)(2,1)} %param.3), kind=kOutput, calls=%fused_computation.5 | convolution fusion | flops 1343225856 | bytes 4718592 | tf_op jit(solution)/shard_map/iap,jbp->ijab/dot_general | solution.py:22
  31.0 0.0 copy-done.3
  31.0 0.0 collective-permute-done
  31.1 0.0 copy-done.2
  31.1 3.2 %convert_bitcast_fusion.1 = bf16[1,1,1024,1024]{2,3,0,1:T(8,128)(2,1)} fusion(bf16[1,1024,640]{2,1,0:T(8,128)(2,1)S(1)} %copy-done.2, bf16[1,1024,640]{2,1,0:T(8,128)(2,1)S(1)} %collective-permute-done), kind=kOutput, calls=%fused_computation.6 | convolution fusion | flops 1343225856 | bytes 4718592 | tf_op jit(solution)/shard_map/iap,jbp->ijab/dot_general | solution.py:22
  34.2 0.0 copy-start
  34.2 0.0 copy-start.4
  34.2 0.0 all-reduce.3.cloned.1.call-update
  35.0 13.2 %collective-permute-start.1 = (bf16[1]{0:T(256)(128)(2,1)}, bf16[1]{0:T(256)(128)(2,1)}, u32[]{:S(2)}, u32[]{:S(2)}) collective-permute-start(bf16[1]{0:T(256)(128)(2,1)} %convert_element_type.44), channel_id=1, source_target_pairs={{0,504},{8,0},{16,8},{24,16},{32,24},{40,32},{48,40},{56,48},{64,5... | collective-permute-start | bytes 14 | tf_op jit(solution)/shard_map/ppermute | solution.py:9
  48.2 2.6 %collective-permute-start.3 = (bf16[1]{0:T(256)(128)(2,1)}, bf16[1]{0:T(256)(128)(2,1)}, u32[]{:S(2)}, u32[]{:S(2)}) collective-permute-start(bf16[1]{0:T(256)(128)(2,1)} %convert_element_type.44), channel_id=1, source_target_pairs={{0,8},{8,16},{16,24},{24,32},{32,40},{40,48},{48,56},{56,64},{64,7... | collective-permute-start | bytes 14 | tf_op jit(solution)/shard_map/ppermute | solution.py:9
  50.8 0.0 collective-permute-done.1
  51.4 2.5 collective-permute-done.3
  54.6 0.0 copy-done
  54.6 191.0 %all-reduce.3.cloned.1.call-done = (bf16[1,1,1024,1024]{2,3,0,1:T(8,128)(2,1)}, bf16[1,1,1024,1024]{2,3,0,1:T(8,128)(2,1)}) async-done(((bf16[1,1,1024,1024]{2,3,0,1:T(8,128)(2,1)}, bf16[1,1,1024,1024]{2,3,0,1:T(8,128)(2,1)}), (bf16[1,1,1024,1024]{2,3,0,1:T(8,128)(2,1)}, bf16[1,1,1024,1024]{2,3,0,1:T(8,128)(2,1)})) %all-reduce.3.cloned.1.call-update) | async-done | bytes 4194320 | tf_op jit(solution)/shard_map/psum | solution.py:23
  245.6 0.0 copy-done.4
  245.6 0.0 copy-start.1
  245.6 3.9 %fusion.2 = f32[1024,640]{1,0:T(8,128)S(1)} fusion(bf16[1,1,1024,1024]{2,3,0,1:T(8,128)(2,1)} %get-tuple-element.5, f32[1024]{0:T(1024)S(1)} %get-tuple-element.8, f32[1024]{0:T(1024)S(1)} %copy-done, bf16[1,1024,640]{2,1,0:T(8,128)(2,1)S(1)} %copy-done.4), kind=kOutput, calls=%fused_computation.7 | convolution fusion | flops 1346371584 | bytes 6037504 | tf_op jit(solution)/shard_map/ijab,jbp->iap/dot_general | solution.py:31
  249.5 0.0 copy-done.1
  249.5 3.6 %add_bitcast_fusion = f32[1,1024,640]{2,1,0:T(8,128)} fusion(f32[1024,640]{1,0:T(8,128)S(1)} %fusion.2, bf16[1,1,1024,1024]{2,3,0,1:T(8,128)(2,1)S(1)} %copy-done.1, f32[1024]{0:T(1024)S(1)} %copy-done, f32[1024]{0:T(1024)S(1)} %get-tuple-element.7, bf16[1,1024,640]{2,1,0:T(8,128)(2,1)S(1)} %collective-permute-done), kind=kOutput, calls=%fused_computation.2 | convolution fusion | flops 1347026944 | bytes 8658944 | tf_op jit(solution)/shard_map/ijab,jbp->iap/dot_general | solution.py:31
  (1 shorter events, 0.0 us)
Async XLA Ops:
  6.5 24.5 %copy-start.2 = (bf16[1,1024,640]{2,1,0:T(8,128)(2,1)S(1)}, bf16[1,1024,640]{2,1,0:T(8,128)(2,1)}, u32[]{:S(2)}) copy-start(bf16[1,1024,640]{2,1,0:T(8,128)(2,1)} %param.3) | copy-start | bytes 3932164
  6.5 239.1 %all-reduce.3.cloned.1.call-start = ((), (), s32[]{:S(2)}) async-start(), calls=%async_computation | async-start | bytes 8388608 | tf_op jit(solution)/shard_map/psum | solution.py:23
  6.5 19.6 %collective-permute-start.2 = (bf16[1,1024,640]{2,1,0:T(8,128)(2,1)}, bf16[1,1024,640]{2,1,0:T(8,128)(2,1)S(1)}, u32[]{:S(2)}, u32[]{:S(2)}) collective-permute-start(bf16[1,1024,640]{2,1,0:T(8,128)(2,1)} %param.3), channel_id=1, source_target_pairs={{0,8},{8,16},{16,24},{24,32},{32,40},{40,48},{48,56},{56,64},{64,7... | collective-permute-start | bytes 3932168 | tf_op jit(solution)/shard_map/ppermute | solution.py:9
  11.3 19.8 %collective-permute-start = (bf16[1,1024,640]{2,1,0:T(8,128)(2,1)}, bf16[1,1024,640]{2,1,0:T(8,128)(2,1)S(1)}, u32[]{:S(2)}, u32[]{:S(2)}) collective-permute-start(bf16[1,1024,640]{2,1,0:T(8,128)(2,1)} %param.3), channel_id=1, source_target_pairs={{0,504},{8,0},{16,8},{24,16},{32,24},{40,32},{48,40},{56,48},{64,5... | collective-permute-start | bytes 3932168 | tf_op jit(solution)/shard_map/ppermute | solution.py:9
  26.1 4.9 %copy-start.3 = (bf16[1,1024,640]{2,1,0:T(8,128)(2,1)}, bf16[1,1024,640]{2,1,0:T(8,128)(2,1)S(1)}, u32[]{:S(2)}) copy-start(bf16[1,1024,640]{2,1,0:T(8,128)(2,1)S(1)} %collective-permute-done.2) | copy-start | bytes 3932164
  34.2 20.4 %copy-start = (f32[1024]{0:T(1024)S(1)}, f32[1024]{0:T(1024)}, u32[]{:S(2)}) copy-start(f32[1024]{0:T(1024)} %param.5) | copy-start | bytes 12292
  34.2 211.4 %copy-start.4 = (bf16[1,1024,640]{2,1,0:T(8,128)(2,1)S(1)}, bf16[1,1024,640]{2,1,0:T(8,128)(2,1)}, u32[]{:S(2)}) copy-start(bf16[1,1024,640]{2,1,0:T(8,128)(2,1)} %copy-done.3) | copy-start | bytes 3932164
  35.0 15.8 %collective-permute-start.1 = (bf16[1]{0:T(256)(128)(2,1)}, bf16[1]{0:T(256)(128)(2,1)}, u32[]{:S(2)}, u32[]{:S(2)}) collective-permute-start(bf16[1]{0:T(256)(128)(2,1)} %convert_element_type.44), channel_id=1, source_target_pairs={{0,504},{8,0},{16,8},{24,16},{32,24},{40,32},{48,40},{56,48},{64,5... | collective-permute-start | bytes 14 | tf_op jit(solution)/shard_map/ppermute | solution.py:9
  48.2 5.7 %collective-permute-start.3 = (bf16[1]{0:T(256)(128)(2,1)}, bf16[1]{0:T(256)(128)(2,1)}, u32[]{:S(2)}, u32[]{:S(2)}) collective-permute-start(bf16[1]{0:T(256)(128)(2,1)} %convert_element_type.44), channel_id=1, source_target_pairs={{0,8},{8,16},{16,24},{24,32},{32,40},{40,48},{48,56},{56,64},{64,7... | collective-permute-start | bytes 14 | tf_op jit(solution)/shard_map/ppermute | solution.py:9
  245.6 3.9 %copy-start.1 = (bf16[1,1,1024,1024]{2,3,0,1:T(8,128)(2,1)S(1)}, bf16[1,1,1024,1024]{2,3,0,1:T(8,128)(2,1)}, u32[]{:S(2)}) copy-start(bf16[1,1,1024,1024]{2,3,0,1:T(8,128)(2,1)} %get-tuple-element.6) | copy-start | bytes 6291460
Sparse Core Ops, SparseCore 0:
  34.4 211.2 all-reduce.2
where the time goes:
time: 260 us
  waiting for transfers between devices  202 us (78%)
  starting transfers between devices  26.6 us (10%)
  matrix products  15.6 us (6%)
  between operations  15.5 us (6%)
    psum x1, waiting for transfers between devices, pair_amplitude(): lax.psum(partial_value.astype(jnp.bfloat16), 'aux').astype(jnp.float32)  191 us
    ppermute x4, starting transfers between devices, from_behind(): lax.ppermute(shard, axis, [(i, (i + by) % count) for i in range(count)])  26.6 us
    ppermute x4, waiting for transfers between devices, from_behind(): lax.ppermute(shard, axis, [(i, (i + by) % count) for i in range(count)])  11.2 us
    dot_general x2, matrix products, pair_amplitude(): jnp.einsum('iap,jbp->ijab', ints_b, other, preferred_element_type=jnp.flo...  8.09 us
    dot_general x2, matrix products, gradient_term(): jnp.einsum('ijab,jbp->iap', amplitude, other, preferred_element_type=jnp....  7.49 us
  transfers between devices with their start and end apart: 5, of which 3 were waited for; matrix products, arithmetic and copies ran while one was open for 2% of the time, Pallas kernels for 0%

commit v1 on v0

v1 whole, which is shorter than its diff:
```python
import functools

import jax
import jax.numpy as jnp
from jax import lax
from jax.experimental import pallas as pl
from jax.experimental.pallas import tpu as pltpu
from jax.sharding import PartitionSpec as P

MESH = pl.DeviceIdType.MESH
NX = 4
PLANE = 16
STEPS = (64, 64, 64, 64)
RELAYED = (1, 3)
ORDER = ('p0', 'p1', 'r0', 'h1', 'p2', 'r1', 'z0', 'h3', 'p3', 'r2', 'z1', 'r3', 'z2', 'z3', 'a0', 'a1', 'f0', 'a2', 'f1', 'g0', 'a3', 'f2', 'g1', 'f3', 'g2', 'g3')
KINDS = (
    "b", "e", "hop", "relay_r", "relay_l", "direct_r", "direct_l", "sum_r", "sum_l", "z", "ag_r", "ag_l", "fw_r", "fw_l", "ret"
)


def kernel(
    ints_ref, energy_ref, virt_hbm, acc, ret_out,
    mine, left_b, hop, virt_ref, part, relay_l, relay_r, direct_l, direct_r, sum_l, sum_r,
    zsend, zrecv, amp, inverse, esend, erecv, ret_send,
    send_sem, recv_sem, local_sem, late_sem,
):
    occ, aux = lax.axis_index("occ"), lax.axis_index("aux")
    n_occ = lax.axis_size("occ")
    x, zh = lax.rem(aux, NX), aux // NX
    xr, xl, xo = lax.rem(x + 1, NX), lax.rem(x + NX - 1, NX), lax.rem(x + 2, NX)
    right, left = (occ, zh * NX + xr), (occ, zh * NX + xl)
    partner = (occ, (1 - zh) * NX + x)
    above, below = (lax.rem(occ + 1, n_occ), aux), (lax.rem(occ + n_occ - 1, n_occ), aux)
    offsets = [sum(STEPS[:s]) for s in range(len(STEPS))]

    load = pltpu.make_async_copy(ints_ref, mine, local_sem.at[0])
    load.start()
    load_virt = pltpu.make_async_copy(virt_hbm, virt_ref, local_sem.at[1])
    load_virt.start()
    energy = energy_ref[0]
    esend[...] = jnp.full(esend.shape, energy, jnp.float32)

    place = lax.rem(occ, PLANE)
    top = place // (PLANE - 1)
    bottom = 1 - (place + PLANE - 1) // PLANE
    next_top = (lax.rem(occ + PLANE, n_occ), aux)
    last_top = (lax.rem(occ + n_occ - PLANE, n_occ), aux)
    first_here = (lax.rem(occ + n_occ - PLANE + 1, n_occ), aux)
    top_here = (lax.rem(occ + PLANE - 1, n_occ), aux)

    def greet(device):
        pl.semaphore_signal(barrier, inc=1, device_id=device, device_id_type=MESH)

    barrier = pltpu.get_barrier_semaphore()
    for device in (right, left, above, below):
        greet(device)

    @pl.when(zh == 0)
    def _():
        greet(partner)

    @pl.when(top == 1)
    def _():
        greet(next_top)
        greet(last_top)
        greet(first_here)

    @pl.when(bottom == 1)
    def _():
        greet(top_here)

    pl.semaphore_wait(barrier, 4 + zh + 3 * top + bottom)

    @pl.when(zh == 1)
    def _():
        pl.semaphore_signal(late_sem, inc=1, device_id=partner, device_id_type=MESH)

    load.wait()

    started = []

    def copy(kind, s, src, dst, device):
        at = KINDS.index(kind)
        return pltpu.make_async_remote_copy(
            src_ref=src, dst_ref=dst, send_sem=send_sem.at[at, s], recv_sem=recv_sem.at[at, s],
            device_id=device, device_id_type=MESH,
        )

    def send(kind, s, src, dst, device, only=None):
        one = copy(kind, s, src, dst, device)
        if only is None:
            one.start()
        else:
            pl.when(only)(one.start)
        started.append((one, only))

    def arrive(kind, s, dst, device):
        copy(kind, s, dst, dst, device).wait_recv()

    def rows(s):
        return pl.ds(offsets[s], STEPS[s])

    def half(s, h):
        return pl.ds(offsets[s] + h * STEPS[s] // 2, STEPS[s] // 2)

    def f32(value):
        return value.astype(jnp.float32)

    send("e", 0, esend, erecv, above)
    for s in range(len(STEPS)):
        if s in RELAYED:
            send("b", s, mine.at[:, rows(s), :], left_b.at[:, rows(s), :], above, top == 0)
            send("hop", s, mine.at[:, rows(s), :], hop.at[:, rows(s), :], next_top, top == 1)
        else:
            send("b", s, mine.at[:, rows(s), :], left_b.at[:, rows(s), :], above)
    load_virt.wait()

    def prepare():
        arrive("e", 0, erecv, below)
        quarter = amp.shape[1]
        column = jnp.broadcast_to(
            virt_ref[0:1, pl.ds(pl.multiple_of(x * quarter, quarter), quarter)], (128, quarter)
        ).T
        row = erecv[0:1, :] + energy - virt_ref[0:1, :]
        inverse[...] = 1.0 / (row - column[:, 0:1])

    def h(s):
        @pl.when(top == 1)
        def _():
            arrive("hop", s, hop.at[:, rows(s), :], last_top)

        send("b", s, hop.at[:, rows(s), :], left_b.at[:, rows(s), :], first_here, top == 1)

    def p(s):
        arrive("b", s, left_b.at[:, rows(s), :], below)
        theirs = left_b[:, rows(s), :].reshape(NX * STEPS[s], -1)
        value = lax.dot_general(
            theirs, mine[...].reshape(-1, mine.shape[-1]), (((1,), (1,)), ((), ())), preferred_element_type=jnp.float32
        )
        part[:, rows(s), :] = value.astype(jnp.bfloat16).reshape(NX, STEPS[s], -1)
        send("relay_r", s, part.at[xo, half(s, 0)], relay_l.at[half(s, 0)], right)
        send("relay_l", s, part.at[xo, half(s, 1)], relay_r.at[half(s, 1)], left)
        send("direct_r", s, part.at[xr, half(s, 1)], direct_l.at[half(s, 1)], right)
        send("direct_l", s, part.at[xl, half(s, 0)], direct_r.at[half(s, 0)], left)

    def r(s):
        arrive("relay_r", s, relay_l.at[half(s, 0)], left)
        relay_l[half(s, 0), :] = (f32(relay_l[half(s, 0), :]) + f32(part[xr, half(s, 0), :])).astype(jnp.bfloat16)
        send("sum_r", s, relay_l.at[half(s, 0)], sum_l.at[half(s, 0)], right)
        arrive("relay_l", s, relay_r.at[half(s, 1)], right)
        relay_r[half(s, 1), :] = (f32(relay_r[half(s, 1), :]) + f32(part[xl, half(s, 1), :])).astype(jnp.bfloat16)
        send("sum_l", s, relay_r.at[half(s, 1)], sum_r.at[half(s, 1)], left)

    def z(s):
        arrive("direct_l", s, direct_r.at[half(s, 0)], right)
        arrive("sum_r", s, sum_l.at[half(s, 0)], left)
        zsend[half(s, 0), :] = (
            f32(part[x, half(s, 0), :]) + f32(sum_l[half(s, 0), :]) + f32(direct_r[half(s, 0), :])
        ).astype(jnp.bfloat16)
        arrive("direct_r", s, direct_l.at[half(s, 1)], left)
        arrive("sum_l", s, sum_r.at[half(s, 1)], right)
        zsend[half(s, 1), :] = (
            f32(part[x, half(s, 1), :]) + f32(sum_r[half(s, 1), :]) + f32(direct_l[half(s, 1), :])
        ).astype(jnp.bfloat16)
        if s == 0:

            @pl.when(zh == 0)
            def _():
                pl.semaphore_wait(late_sem, 1)

        send("z", s, zsend.at[rows(s)], zrecv.at[rows(s)], partner)

    def a(s):
        if s == 0:
            prepare()
        arrive("z", s, zrecv.at[rows(s)], partner)
        coulomb = f32(zsend[rows(s), :]) + f32(zrecv[rows(s), :])
        amp[x, rows(s), :] = (coulomb * inverse[rows(s), :]).astype(jnp.bfloat16)
        send("ag_r", s, amp.at[x, rows(s)], amp.at[x, rows(s)], right)
        send("ag_l", s, amp.at[x, rows(s)], amp.at[x, rows(s)], left)

    def f(s):
        arrive("ag_r", s, amp.at[xl, rows(s)], left)
        send("fw_r", s, amp.at[xl, half(s, 0)], amp.at[xl, half(s, 0)], right)
        arrive("ag_l", s, amp.at[xr, rows(s)], right)
        send("fw_l", s, amp.at[xr, half(s, 1)], amp.at[xr, half(s, 1)], left)

    def g(s):
        arrive("fw_r", s, amp.at[xo, half(s, 0)], left)
        arrive("fw_l", s, amp.at[xo, half(s, 1)], right)
        block = amp[:, rows(s), :].reshape(NX * STEPS[s], -1)
        back = jnp.dot(block, mine[...].reshape(-1, mine.shape[-1]), preferred_element_type=jnp.float32)
        ret_send[:, rows(s), :] = back.astype(jnp.bfloat16).reshape(NX, STEPS[s], -1)
        send("ret", s, ret_send.at[:, rows(s), :], ret_out.at[:, rows(s), :], below)
        theirs = left_b[:, rows(s), :].reshape(NX * STEPS[s], -1)
        own = lax.dot_general(block, theirs, (((0,), (0,)), ((), ())), preferred_element_type=jnp.float32)
        if s == 0:
            acc[...] = own
        else:
            acc[...] += own

    act = {"h": h, "p": p, "r": r, "z": z, "a": a, "f": f, "g": g}
    for item in ORDER:
        act[item[0]](int(item[1:]))

    for s in range(len(STEPS)):
        arrive("ret", s, ret_out.at[:, rows(s), :], above)
    for one, only in started:
        if only is None:
            one.wait_send()
        else:
            pl.when(only)(one.wait_send)


def per_device(ints_b, occ_energy, virt_energy):
    _, virt, naux = ints_b.shape
    quarter = virt // NX
    bf16, f32 = jnp.bfloat16, jnp.float32
    steps = len(STEPS)
    hbm, vmem = pl.BlockSpec(memory_space=pltpu.HBM), pl.BlockSpec(memory_space=pltpu.VMEM)
    slab = pltpu.VMEM((quarter, virt), bf16)
    kept, returned = pl.pallas_call(
        kernel,
        out_shape=(jax.ShapeDtypeStruct((virt, naux), f32), jax.ShapeDtypeStruct((NX, quarter, naux), bf16)),
        in_specs=[hbm, pl.BlockSpec(memory_space=pltpu.SMEM), hbm],
        out_specs=(vmem, vmem),
        scratch_shapes=[
            pltpu.VMEM((NX, quarter, naux), bf16),
            pltpu.VMEM((NX, quarter, naux), bf16),
            pltpu.VMEM((NX, quarter, naux), bf16),
            pltpu.VMEM((1, virt), f32),
            pltpu.VMEM((NX, quarter, virt), bf16),
            slab, slab, slab, slab, slab, slab,
            slab, slab,
            pltpu.VMEM((NX, quarter, virt), bf16),
            pltpu.VMEM((quarter, virt), f32),
            pltpu.VMEM((8, virt), f32),
            pltpu.VMEM((8, virt), f32),
            pltpu.VMEM((NX, quarter, naux), bf16),
            pltpu.SemaphoreType.DMA((len(KINDS), steps)),
            pltpu.SemaphoreType.DMA((len(KINDS), steps)),
            pltpu.SemaphoreType.DMA((2,)),
            pltpu.SemaphoreType.REGULAR,
        ],
        compiler_params=pltpu.CompilerParams(collective_id=0, has_side_effects=True, vmem_limit_bytes=48 * 2**20),
        cost_estimate=pl.CostEstimate(flops=6 * virt * virt * naux, bytes_accessed=10 * virt * naux, transcendentals=0),
        name="pair_gradient",
    )(ints_b.reshape(NX, quarter, naux), occ_energy, virt_energy.reshape(1, virt))
    total = kept + returned.reshape(virt, naux).astype(f32)
    return total.reshape(1, virt, naux)


def solution(mesh):
    placed = (P("occ", None, "aux"), P("occ"), P())
    return jax.shard_map(
        per_device, mesh=mesh, in_specs=placed, out_specs=P("occ", None, "aux"), check_vma=False
    )
```

time: 260 us -> 73 us (0.28)
  waiting for transfers between devices: 202 us -> 0 us
  Pallas kernels: 0 us -> 68.3 us
  starting transfers between devices: 26.6 us -> 0 us
  matrix products: 15.6 us -> 0 us
  between operations: 15.5 us -> 0.67 us
    psum x1 -> x0, waiting for transfers between devices: 191 us -> none  [pair_amplitude(): lax.psum(partial_value.astype(jnp.bfloat16), 'aux').astype(jnp.float32)]
    pallas_call x0 -> x1, Pallas kernels: none -> 68.3 us  [per_device(): pl.pallas_call(kernel, out_shape=(jax.ShapeDtypeStruct((virt, naux), f32)...]
    ppermute x4 -> x0, starting transfers between devices: 26.6 us -> none  [from_behind(): lax.ppermute(shard, axis, [(i, (i + by) % count) for i in range(count)])]
    dot_general x4 -> x0, matrix products: 15.6 us -> none  [the longest x2 8.09 us: pair_amplitude(): jnp.einsum('iap,jbp->ijab', ints_b, other, preferred_element_type=jnp.flo...]
    ppermute x4 -> x0, waiting for transfers between devices: 11.2 us -> none  [from_behind(): lax.ppermute(shard, axis, [(i, (i + by) % count) for i in range(count)])]
  transfers between devices with their start and end apart: 5 -> 0, of which waited for: 3 -> 0; matrix products, arithmetic and copies ran while one was open for 2% -> 0% of each run, Pallas kernels for 0% -> 0%
where the time goes in v1:
time: 73 us; the launch traced here: 72.8 us
  Pallas kernels  68.3 us (94%)
  local copies, waits for them, and re-layouts  2 us (3%)
  other arithmetic  1.87 us (3%)
    pallas_call x1, Pallas kernels, per_device(): pl.pallas_call(kernel, out_shape=(jax.ShapeDtypeStruct((virt, naux), f32)...  68.3 us
    unnamed x4, local copies, waits for them, and re-layouts  2 us
    reshape x1, other arithmetic, per_device(): return total.reshape(1, virt, naux)  1.87 us

profile of v1, /device:TPU:1, one launch (start us, length us, event | category | flops | bytes accessed | tf_op | source)
XLA Modules:
  0.0 72.8 jit_solution(7186989768002797952)
XLA Ops:
  0.7 0.0 copy-start
  0.7 1.3 %copy-done = bf16[1,1024,640]{2,1,0:T(8,128)(2,1)S(1)} copy-done((bf16[1,1024,640]{2,1,0:T(8,128)(2,1)S(1)}, bf16[1,1024,640]{2,1,0:T(8,128)(2,1)}, u32[]{:S(2)}) %copy-start) | copy-done | bytes 1310744
  2.0 0.0 copy-start.1
  2.0 0.7 copy-done.1
  2.7 68.3 %pair_gradient.1 = (f32[1024,640]{1,0:T(8,128)S(1)}, bf16[4,256,640]{2,1,0:T(8,128)(2,1)S(1)}) custom-call(bf16[4,256,640]{2,1,0:T(8,128)(2,1)S(1)} %bitcast.7, f32[1]{0:T(128)S(6)} %copy.4.energy_ref, f32[1,1024]{1,0:T(1,128)S(1)} %bitcast.8), custom_call_target="tpu_custom_call" | custom-call | flops 4026531840 | bytes 6553600 | tf_op jit(solution)/shard_map/pair_gradient/pallas_call | solution.py:222
  70.9 1.9 %fusion = f32[1,1024,640]{2,1,0:T(8,128)} fusion(f32[1024,640]{1,0:T(8,128)S(1)} %get-tuple-element.7, bf16[4,256,640]{2,1,0:T(8,128)(2,1)S(1)} %get-tuple-element.8), kind=kLoop, calls=%fused_computation.1 | loop fusion | flops 1310720 | bytes 6553600 | tf_op jit(solution)/shard_map/reshape | solution.py:250
Async XLA Ops:
  0.7 1.3 %copy-start = (bf16[1,1024,640]{2,1,0:T(8,128)(2,1)S(1)}, bf16[1,1024,640]{2,1,0:T(8,128)(2,1)}, u32[]{:S(2)}) copy-start(bf16[1,1024,640]{2,1,0:T(8,128)(2,1)} %param.3) | copy-start | bytes 3932164
  2.0 0.7 copy-start.1

commit v2 on v1

--- a/solution.py
+++ b/solution.py
@@ -8,20 +8,22 @@
 from jax.sharding import PartitionSpec as P
 
 MESH = pl.DeviceIdType.MESH
+ADD_PIECES = 4
 NX = 4
 PLANE = 16
-STEPS = (64, 64, 64, 64)
-RELAYED = (1, 3)
-ORDER = ('p0', 'p1', 'r0', 'h1', 'p2', 'r1', 'z0', 'h3', 'p3', 'r2', 'z1', 'r3', 'z2', 'z3', 'a0', 'a1', 'f0', 'a2', 'f1', 'g0', 'a3', 'f2', 'g1', 'f3', 'g2', 'g3')
+STEPS = (64, 64, 64, 32, 32)
+RELAYED = (1, 2, 4)
+ORDER = ('p0', 'p1', 'r0', 'h1', 'p2', 'r1', 'z0', 'h2', 'p3', 'r2', 'z1', 'h4', 'p4', 'r3', 'z2', 'r4', 'z3', 'z4', 'a0', 'a1', 'f0', 'a2', 'f1', 'g0', 'a3', 'f2', 'g1', 'a4', 'f3', 'g2', 'f4', 'g3', 'k4', 'g4', 'q0')
 KINDS = (
-    "b", "e", "hop", "relay_r", "relay_l", "direct_r", "direct_l", "sum_r", "sum_l", "z", "ag_r", "ag_l", "fw_r", "fw_l", "ret"
+    "b", "e", "hop", "relay_r", "relay_l", "direct_r", "direct_l", "sum_r", "sum_l", "z", "ag_r", "ag_l", "fw_r", "fw_l", "ret",
+    "ret_own", "ret_l", "ret_r",
 )
 
 
 def kernel(
-    ints_ref, energy_ref, virt_hbm, acc, ret_out,
+    ints_ref, energy_ref, virt_hbm, acc_out, ret_out,
     mine, left_b, hop, virt_ref, part, relay_l, relay_r, direct_l, direct_r, sum_l, sum_r,
-    zsend, zrecv, amp, inverse, esend, erecv, ret_send,
+    zsend, zrecv, amp, inverse, esend, erecv, ret_send, acc,
     send_sem, recv_sem, local_sem, late_sem,
 ):
     occ, aux = lax.axis_index("occ"), lax.axis_index("aux")
@@ -48,6 +50,8 @@
     first_here = (lax.rem(occ + n_occ - PLANE + 1, n_occ), aux)
     top_here = (lax.rem(occ + PLANE - 1, n_occ), aux)
 
+    is_top, not_top = top == 1, top == 0
+
     def greet(device):
         pl.semaphore_signal(barrier, inc=1, device_id=device, device_id_type=MESH)
 
@@ -59,7 +63,7 @@
     def _():
         greet(partner)
 
-    @pl.when(top == 1)
+    @pl.when(is_top)
     def _():
         greet(next_top)
         greet(last_top)
@@ -77,7 +81,8 @@
 
     load.wait()
 
-    started = []
+    started = {}
+    first = {}
 
     def copy(kind, s, src, dst, device):
         at = KINDS.index(kind)
@@ -92,7 +97,7 @@
             one.start()
         else:
             pl.when(only)(one.start)
-        started.append((one, only))
+        started[kind, s, only is is_top] = (src, dst, device, only)
 
     def arrive(kind, s, dst, device):
         copy(kind, s, dst, dst, device).wait_recv()
@@ -109,8 +114,8 @@
     send("e", 0, esend, erecv, above)
     for s in range(len(STEPS)):
         if s in RELAYED:
-            send("b", s, mine.at[:, rows(s), :], left_b.at[:, rows(s), :], above, top == 0)
-            send("hop", s, mine.at[:, rows(s), :], hop.at[:, rows(s), :], next_top, top == 1)
+            send("b", s, mine.at[:, rows(s), :], left_b.at[:, rows(s), :], above, not_top)
+            send("hop", s, mine.at[:, rows(s), :], hop.at[:, rows(s), :], next_top, is_top)
         else:
             send("b", s, mine.at[:, rows(s), :], left_b.at[:, rows(s), :], above)
     load_virt.wait()
@@ -125,11 +130,11 @@
         inverse[...] = 1.0 / (row - column[:, 0:1])
 
     def h(s):
-        @pl.when(top == 1)
+        @pl.when(is_top)
         def _():
             arrive("hop", s, hop.at[:, rows(s), :], last_top)
 
-        send("b", s, hop.at[:, rows(s), :], left_b.at[:, rows(s), :], first_here, top == 1)
+        send("b", s, hop.at[:, rows(s), :], left_b.at[:, rows(s), :], first_here, is_top)
 
     def p(s):
         arrive("b", s, left_b.at[:, rows(s), :], below)
@@ -151,7 +156,7 @@
         relay_r[half(s, 1), :] = (f32(relay_r[half(s, 1), :]) + f32(part[xl, half(s, 1), :])).astype(jnp.bfloat16)
         send("sum_l", s, relay_r.at[half(s, 1)], sum_r.at[half(s, 1)], left)
 
-    def z(s):
+    def sum_halves(s):
         arrive("direct_l", s, direct_r.at[half(s, 0)], right)
         arrive("sum_r", s, sum_l.at[half(s, 0)], left)
         zsend[half(s, 0), :] = (
@@ -162,7 +167,10 @@
         zsend[half(s, 1), :] = (
             f32(part[x, half(s, 1), :]) + f32(sum_r[half(s, 1), :]) + f32(direct_l[half(s, 1), :])
         ).astype(jnp.bfloat16)
-        if s == 0:
+
+    def z(s):
+        sum_halves(s)
+        if s == first["z"]:
 
             @pl.when(zh == 0)
             def _():
@@ -171,7 +179,7 @@
         send("z", s, zsend.at[rows(s)], zrecv.at[rows(s)], partner)
 
     def a(s):
-        if s == 0:
+        if s == first["a"]:
             prepare()
         arrive("z", s, zrecv.at[rows(s)], partner)
         coulomb = f32(zsend[rows(s), :]) + f32(zrecv[rows(s), :])
@@ -185,31 +193,84 @@
         arrive("ag_l", s, amp.at[xr, rows(s)], right)
         send("fw_l", s, amp.at[xr, half(s, 1)], amp.at[xr, half(s, 1)], left)
 
+    split = [int(item[1:]) for item in ORDER if item[0] == "k"]
+    quarters = (("ret_own", x), ("ret_l", xl), ("ret_r", xr), ("ret", xo))
+
+    def give_back(kind, s, at):
+        back = jnp.dot(amp[at, rows(s), :], mine[...].reshape(-1, mine.shape[-1]), preferred_element_type=jnp.float32)
+        ret_send[at, rows(s), :] = back.astype(jnp.bfloat16)
+        send(kind, s, ret_send.at[at, rows(s)], ret_out.at[at, rows(s)], below)
+
+    def k(s):
+        for kind, at in quarters[:3]:
+            give_back(kind, s, at)
+
     def g(s):
         arrive("fw_r", s, amp.at[xo, half(s, 0)], left)
         arrive("fw_l", s, amp.at[xo, half(s, 1)], right)
-        block = amp[:, rows(s), :].reshape(NX * STEPS[s], -1)
-        back = jnp.dot(block, mine[...].reshape(-1, mine.shape[-1]), preferred_element_type=jnp.float32)
-        ret_send[:, rows(s), :] = back.astype(jnp.bfloat16).reshape(NX, STEPS[s], -1)
-        send("ret", s, ret_send.at[:, rows(s), :], ret_out.at[:, rows(s), :], below)
-        theirs = left_b[:, rows(s), :].reshape(NX * STEPS[s], -1)
-        own = lax.dot_general(block, theirs, (((0,), (0,)), ((), ())), preferred_element_type=jnp.float32)
-        if s == 0:
-            acc[...] = own
-        else:
-            acc[...] += own
-
-    act = {"h": h, "p": p, "r": r, "z": z, "a": a, "f": f, "g": g}
-    for item in ORDER:
-        act[item[0]](int(item[1:]))
+        if s in split:
+            give_back("ret", s, xo)
+        else:
+            block = amp[:, rows(s), :].reshape(NX * STEPS[s], -1)
+            back = jnp.dot(block, mine[...].reshape(-1, mine.shape[-1]), preferred_element_type=jnp.float32)
+            ret_send[:, rows(s), :] = back.astype(jnp.bfloat16).reshape(NX, STEPS[s], -1)
+            send("ret", s, ret_send.at[:, rows(s), :], ret_out.at[:, rows(s), :], below)
+
+    def q(_):
+        virt = NX * amp.shape[1]
+        acc[...] = lax.dot_general(
+            amp[...].reshape(virt, virt), left_b[...].reshape(virt, -1), (((0,), (0,)), ((), ())),
+            preferred_element_type=jnp.float32,
+        )
+
+    act = {"h": h, "p": p, "r": r, "z": z, "a": a, "f": f, "k": k, "g": g, "q": q}
+
+    def run(order):
+        for item in reversed(order):
+            first[item[0]] = int(item[1:])
+        for item in order:
+            act[item[0]](int(item[1:]))
+
+    run(ORDER)
+    store = pltpu.make_async_copy(acc, acc_out, local_sem.at[2])
+    store.start()
 
     for s in range(len(STEPS)):
-        arrive("ret", s, ret_out.at[:, rows(s), :], above)
-    for one, only in started:
+        if s in split:
+            for kind, at in quarters:
+                arrive(kind, s, ret_out.at[at, rows(s)], above)
+        else:
+            arrive("ret", s, ret_out.at[:, rows(s), :], above)
+    for (kind, s, _), (src, dst, device, only) in started.items():
         if only is None:
-            one.wait_send()
-        else:
-            pl.when(only)(one.wait_send)
+            copy(kind, s, src, dst, device).wait_send()
+        else:
+            pl.when(only)(copy(kind, s, src, dst, device).wait_send)
+    store.wait()
+
+
+def add(kept_ref, returned_ref, out_ref, total, returned, sem):
+    rows = total.shape[0] // ADD_PIECES
+    pieces = [pl.ds(i * rows, rows) for i in range(ADD_PIECES)]
+    loads = [
+        (
+            pltpu.make_async_copy(kept_ref.at[at], total.at[at], sem.at[0, i]),
+            pltpu.make_async_copy(returned_ref.at[at], returned.at[at], sem.at[1, i]),
+        )
+        for i, at in enumerate(pieces)
+    ]
+    for pair in loads:
+        for one in pair:
+            one.start()
+    stores = []
+    for i, at in enumerate(pieces):
+        for one in loads[i]:
+            one.wait()
+        total[at, :] += returned[at, :].astype(jnp.float32)
+        stores.append(pltpu.make_async_copy(total.at[at], out_ref.at[at], sem.at[2, i]))
+        stores[i].start()
+    for one in stores:
+        one.wait()
 
 
 def per_device(ints_b, occ_energy, virt_energy):
@@ -223,7 +284,7 @@
         kernel,
         out_shape=(jax.ShapeDtypeStruct((virt, naux), f32), jax.ShapeDtypeStruct((NX, quarter, naux), bf16)),
         in_specs=[hbm, pl.BlockSpec(memory_space=pltpu.SMEM), hbm],
-        out_specs=(vmem, vmem),
+        out_specs=(hbm, hbm),
         scratch_shapes=[
             pltpu.VMEM((NX, quarter, naux), bf16),
             pltpu.VMEM((NX, quarter, naux), bf16),
@@ -237,16 +298,29 @@
             pltpu.VMEM((8, virt), f32),
             pltpu.VMEM((8, virt), f32),
             pltpu.VMEM((NX, quarter, naux), bf16),
+            pltpu.VMEM((virt, naux), f32),
             pltpu.SemaphoreType.DMA((len(KINDS), steps)),
             pltpu.SemaphoreType.DMA((len(KINDS), steps)),
-            pltpu.SemaphoreType.DMA((2,)),
+            pltpu.SemaphoreType.DMA((3,)),
             pltpu.SemaphoreType.REGULAR,
         ],
-        compiler_params=pltpu.CompilerParams(collective_id=0, has_side_effects=True, vmem_limit_bytes=48 * 2**20),
+        compiler_params=pltpu.CompilerParams(collective_id=0, has_side_effects=True, vmem_limit_bytes=56 * 2**20),
         cost_estimate=pl.CostEstimate(flops=6 * virt * virt * naux, bytes_accessed=10 * virt * naux, transcendentals=0),
         name="pair_gradient",
     )(ints_b.reshape(NX, quarter, naux), occ_energy, virt_energy.reshape(1, virt))
-    total = kept + returned.reshape(virt, naux).astype(f32)
+    total = pl.pallas_call(
+        add,
+        out_shape=jax.ShapeDtypeStruct((virt, naux), f32),
+        in_specs=[hbm, hbm],
+        out_specs=hbm,
+        scratch_shapes=[
+            pltpu.VMEM((virt, naux), f32),
+            pltpu.VMEM((virt, naux), bf16),
+            pltpu.SemaphoreType.DMA((3, ADD_PIECES)),
+        ],
+        compiler_params=pltpu.CompilerParams(vmem_limit_bytes=56 * 2**20),
+        name="add_returned",
+    )(kept, returned.reshape(virt, naux))
     return total.reshape(1, virt, naux)
 
 

time: 73 us -> 71.8 us (0.984)
  the two profiles are of different devices: /device:TPU:1 before, /device:TPU:49 now
where the time goes in v2:
time: 71.8 us; the launch traced here: 71.7 us
  Pallas kernels  71 us (99%)
    pallas_call x1, Pallas kernels, per_device(): pl.pallas_call(kernel, out_shape=(jax.ShapeDtypeStruct((virt, naux), f32)...  67.9 us
    pallas_call x1, Pallas kernels, per_device(): pl.pallas_call(add, out_shape=jax.ShapeDtypeStruct((virt, naux), f32), in...  3.05 us

profile of v2, /device:TPU:49, one launch (start us, length us, event | category | flops | bytes accessed | tf_op | source)
XLA Modules:
  0.0 71.7 jit_solution(11658822846134719557)
XLA Ops:
  0.7 67.9 %pair_gradient.1 = (f32[1024,640]{1,0:T(8,128)}, bf16[4,256,640]{2,1,0:T(8,128)(2,1)}) custom-call(bf16[4,256,640]{2,1,0:T(8,128)(2,1)} %bitcast.5, f32[1]{0:T(128)S(6)} %copy.4.energy_ref, f32[1,1024]{1,0:T(1,128)} %bitcast.6), custom_call_target="tpu_custom_call" | custom-call | flops 4026531840 | bytes 6553600 | tf_op jit(solution)/shard_map/pair_gradient/pallas_call | solution.py:283
  68.6 3.1 %add_returned.1 = f32[1024,640]{1,0:T(8,128)} custom-call(f32[1024,640]{1,0:T(8,128)} %get-tuple-element.7.kept_ref, bf16[1024,640]{1,0:T(8,128)(2,1)} %bitcast.4), custom_call_target="tpu_custom_call" | custom-call | tf_op jit(solution)/shard_map/add_returned/pallas_call | solution.py:311

commit v3 on v2

--- a/solution.py
+++ b/solution.py
@@ -13,7 +13,7 @@
 PLANE = 16
 STEPS = (64, 64, 64, 32, 32)
 RELAYED = (1, 2, 4)
-ORDER = ('p0', 'p1', 'r0', 'h1', 'p2', 'r1', 'z0', 'h2', 'p3', 'r2', 'z1', 'h4', 'p4', 'r3', 'z2', 'r4', 'z3', 'z4', 'a0', 'a1', 'f0', 'a2', 'f1', 'g0', 'a3', 'f2', 'g1', 'a4', 'f3', 'g2', 'f4', 'g3', 'k4', 'g4', 'q0')
+ORDER = ('p0', 'p1', 'e0', 'r0', 'h1', 'p2', 'r1', 'z0', 'h2', 'p3', 'r2', 'z1', 'h4', 'p4', 'r3', 'z2', 'r4', 'z3', 'z4', 'a0', 'a1', 'f0', 'a2', 'f1', 'g0', 'a3', 'f2', 'g1', 'a4', 'f3', 'g2', 'f4', 'g3', 'k4', 'g4', 'q0')
 KINDS = (
     "b", "e", "hop", "relay_r", "relay_l", "direct_r", "direct_l", "sum_r", "sum_l", "z", "ag_r", "ag_l", "fw_r", "fw_l", "ret",
     "ret_own", "ret_l", "ret_r",
@@ -120,7 +120,7 @@
             send("b", s, mine.at[:, rows(s), :], left_b.at[:, rows(s), :], above)
     load_virt.wait()
 
-    def prepare():
+    def prepare(_):
         arrive("e", 0, erecv, below)
         quarter = amp.shape[1]
         column = jnp.broadcast_to(
@@ -179,8 +179,6 @@
         send("z", s, zsend.at[rows(s)], zrecv.at[rows(s)], partner)
 
     def a(s):
-        if s == first["a"]:
-            prepare()
         arrive("z", s, zrecv.at[rows(s)], partner)
         coulomb = f32(zsend[rows(s), :]) + f32(zrecv[rows(s), :])
         amp[x, rows(s), :] = (coulomb * inverse[rows(s), :]).astype(jnp.bfloat16)
@@ -223,7 +221,7 @@
             preferred_element_type=jnp.float32,
         )
 
-    act = {"h": h, "p": p, "r": r, "z": z, "a": a, "f": f, "k": k, "g": g, "q": q}
+    act = {"e": prepare, "h": h, "p": p, "r": r, "z": z, "a": a, "f": f, "k": k, "g": g, "q": q}
 
     def run(order):
         for item in reversed(order):

time: 71.8 us -> 71.8 us (level)
  no operation moved by 1% of the time
where the time goes in v3:
time: 71.8 us; the launch traced here: 71.7 us
  Pallas kernels  71 us (99%)
    pallas_call x1, Pallas kernels, per_device(): pl.pallas_call(kernel, out_shape=(jax.ShapeDtypeStruct((virt, naux), f32)...  67.9 us
    pallas_call x1, Pallas kernels, per_device(): pl.pallas_call(add, out_shape=jax.ShapeDtypeStruct((virt, naux), f32), in...  3.05 us

profile of v3, /device:TPU:49, one launch (start us, length us, event | category | flops | bytes accessed | tf_op | source)
XLA Modules:
  0.0 71.7 jit_solution(16913884499415203173)
XLA Ops:
  0.7 67.9 %pair_gradient.1 = (f32[1024,640]{1,0:T(8,128)}, bf16[4,256,640]{2,1,0:T(8,128)(2,1)}) custom-call(bf16[4,256,640]{2,1,0:T(8,128)(2,1)} %bitcast.5, f32[1]{0:T(128)S(6)} %copy.4.energy_ref, f32[1,1024]{1,0:T(1,128)} %bitcast.6), custom_call_target="tpu_custom_call" | custom-call | flops 4026531840 | bytes 6553600 | tf_op jit(solution)/shard_map/pair_gradient/pallas_call | solution.py:281
  68.6 3.1 %add_returned.1 = f32[1024,640]{1,0:T(8,128)} custom-call(f32[1024,640]{1,0:T(8,128)} %get-tuple-element.7.kept_ref, bf16[1024,640]{1,0:T(8,128)(2,1)} %bitcast.4), custom_call_target="tpu_custom_call" | custom-call | tf_op jit(solution)/shard_map/add_returned/pallas_call | solution.py:309
